TPU v7x, 256 devices: a whole 4x4x8 slice. The times are simulated.
256 devices in a mesh: cuts: 32 (over z, x_hi, core), band: 8 (over x_lo, y).
Axes of the slice: x: 4 (x_hi: 2, x_lo: 2; x = x_hi * 2 + x_lo), y: 4, z: 8, core: 2. Of those that a mesh axis runs over, the one named last changes fastest.
Arguments:
- eigvecs: bfloat16 [6144, 114688], P('band', 'cuts'), may hold values from -0.3984375 to 0.3984375
- energies: float32 [114688], P('cuts'), may hold values from -1 to 1
- smearing: float32 [114688], P('cuts'), may hold values from 0.05 to 1
- counts: int32 [64], P('cuts'), may hold values from 298 to 1792, as said below
- occupied: int32 [64], P('cuts'), may hold values from 1 to 1568, as said below
- block_cols: int32 [48, 3], P('band'), may hold values from 0 to 47, as said below
Outputs:
- density: float32 [6144, 384], P(('band', 'cuts'))
- energy_density: float32 [6144, 384], P(('band', 'cuts'))
Inputs may be any that keep to these rules, and one draw needn't show every extreme that they name: `counts`: each slice has between 298 and 1792 eigenvectors; some slice has exactly 1792, some exactly 298. `occupied`: at least one and at most the slice's count, and at most 1568; both ends are reached. `block_cols`: row I holds I first, then two distinct block indices other than I that lie within 2 of I.
All inputs are finite; a program needn't handle non-finite values.
Results may differ from a plain program's by a relative error of at most 0.0029.
Values may be sent and summed in bfloat16 or wider, within the bound.
A program may use at most 128 MiB of HBM per device.

v0:
```python
import jax
import jax.numpy as jnp
from jax import lax
from jax.sharding import PartitionSpec as P

BS = 128
PANEL = 128
COLS = 1792


def with_halo(array, sides, width):
    for axis, dim in sides:
        count, length = (lax.axis_size(axis), array.shape[dim])
        up = [(i, (i + 1) % count) for i in range(count - 1)]
        down = [(j, i) for i, j in up]
        last = lax.slice_in_dim(array, length - width, length, axis=dim)
        initial = lax.slice_in_dim(array, 0, width, axis=dim)
        before = lax.ppermute(last, axis, up)
        after = lax.ppermute(initial, axis, down)
        array = jnp.concatenate([before, array, after], axis=dim)
    return array


def live_panels(slice_counts, panels, per_slice):
    panel_ids = jnp.arange(panels, dtype=jnp.int32)
    return panel_ids % per_slice * PANEL < slice_counts[panel_ids // per_slice]


def shards(eigvecs, energies, smearing, counts, occupied, block_cols):
    rows, cols = eigvecs.shape
    nblocks = rows // BS
    stored = block_cols.shape[1]
    per_slice = COLS // PANEL
    panels = cols // PANEL
    slot = jnp.arange(cols, dtype=jnp.int32)
    owner_slice = slot // COLS
    within = slot % COLS
    count_col = counts[owner_slice]
    occ_col = occupied[owner_slice]
    weight = jnp.where(
        within < count_col,
        jnp.where(within < occ_col, jnp.float32(2.0), smearing),
        jnp.float32(0.0),
    )
    weight_energy = weight * energies
    weight_panels = weight.reshape(panels, PANEL)
    energy_panels = weight_energy.reshape(panels, PANEL)
    padded = with_halo(eigvecs, (("band", 0),), 2 * BS)
    first_block = lax.axis_index("band") * nblocks
    row_index = ((block_cols - first_block + 2) * BS)[:, :, None] + jnp.arange(BS, dtype=jnp.int32)[
        None, None, :
    ]

    def add_terms(totals, pad_panel, w_panel, we_panel):
        own_panel = lax.dynamic_slice_in_dim(pad_panel, 2 * BS, rows, 0)
        wide = pad_panel.astype(jnp.float32)
        scaled = (wide * w_panel[None, :]).astype(jnp.bfloat16)
        scaled_e = (wide * we_panel[None, :]).astype(jnp.bfloat16)
        far_panel = scaled[row_index]
        far_panel_e = scaled_e[row_index]
        own_three = own_panel.reshape(nblocks, BS, PANEL)
        dens = jnp.einsum(
            "bik,bjck->bijc", own_three, far_panel, preferred_element_type=jnp.float32
        )
        edens = jnp.einsum(
            "bik,bjck->bijc", own_three, far_panel_e, preferred_element_type=jnp.float32
        )
        return (totals[0] + dens, totals[1] + edens)

    live = live_panels(counts, panels, per_slice)
    live_int = live.astype(jnp.int32)
    load = jnp.sum(live_int)
    rank = jnp.cumsum(live_int) - live_int

    def add_own(step, totals):

        def compute(kept):
            pad_panel = lax.dynamic_slice_in_dim(padded, step * PANEL, PANEL, 1)
            w_panel = lax.dynamic_index_in_dim(weight_panels, step, 0, False)
            we_panel = lax.dynamic_index_in_dim(energy_panels, step, 0, False)
            return add_terms(kept, pad_panel, w_panel, we_panel)

        return lax.cond(live[step] & (rank[step] < load), compute, lambda kept: kept, totals)

    zeros = jnp.zeros((nblocks, BS, stored, BS), jnp.float32)
    totals = lax.fori_loop(0, panels, add_own, (zeros, zeros))
    dens = totals[0].reshape(rows, stored * BS)
    edens = totals[1].reshape(rows, stored * BS)
    density, energy_density = (
        lax.psum_scatter(dens, "cuts", scatter_dimension=0, tiled=True),
        lax.psum_scatter(edens, "cuts", scatter_dimension=0, tiled=True),
    )
    return (density, energy_density)


def solution(mesh):
    placed = (P("band", "cuts"), P("cuts"), P("cuts"), P("cuts"), P("cuts"), P("band", None))
    return jax.shard_map(
        shards,
        mesh=mesh,
        in_specs=placed,
        out_specs=(P(("band", "cuts"), None), P(("band", "cuts"), None)),
        check_vma=False,
    )
```

profile of v0, /device:TPU:1, one launch (start us, length us, event | category | flops | bytes accessed | tf_op | source)
XLA Modules:
  0.0 861.8 jit_solution(5036345620682347452)
XLA Ops:
  24.3 30.0 %collective-permute-done = bf16[256,3584]{1,0:T(8,128)(2,1)S(1)} collective-permute-done((bf16[256,3584]{1,0:T(8,128)(2,1)}, bf16[256,3584]{1,0:T(8,128)(2,1)S(1)}, u32[]{:S(2)}, u32[]{:S(2)}) %collective-permute-start) | collective-permute-done | bytes 1835040 | tf_op jit(solution)/shard_map/ppermute | solution.py:18
  58.3 7.0 pad_maximum_fusion
  66.6 352.2 %while.16 = (s32[]{:T(128)}, f32[6,128,3,128]{3,1,2,0:T(8,128)S(1)}, f32[6,128,3,128]{3,1,2,0:T(8,128)}, pred[28]{0:T(512)(128)(4,1)S(1)}, s32[28]{0:T(128)S(1)}...) while((s32[]{:T(128)}, ...), condition=%wide.region_5.6_spmd.clone, body=%wide.region_2.5_spmd.clone.sunk | while | flops 152416256 | bytes 10116520 | solution.py:86
  69.6 14.7 %conditional.3 = ((f32[6,128,3,128]{3,1,2,0:T(8,128)S(1)}, f32[6,128,3,128]{3,1,2,0:T(8,128)})) conditional(s32[]{:T(128)} %convert_element_type.43, (f32[6,128,3,128]{3,1,2,0:T(8,128)S(1)}, f32[6,128,3,128]{3,1,2,0:T(8,128)}) %tuple.56, (s32[]{:T(128)}, bf16[1280,3584]{1,0:T(8,128)(2,1)}, f32[28,128]{1,0:T(8,128)S(1)}, s32[6,3]{1,0:T(8,128)S(1)}, ...), branch_computations={%region_3.3_spmd, %region_4.4_spmd} | conditional | flops 152416256 | bytes 10107080 | solution.py:83
  70.9 4.7 gather_fusion.1
  87.5 14.7 %conditional.3 = ((f32[6,128,3,128]{3,1,2,0:T(8,128)S(1)}, f32[6,128,3,128]{3,1,2,0:T(8,128)})) conditional(s32[]{:T(128)} %convert_element_type.43, (f32[6,128,3,128]{3,1,2,0:T(8,128)S(1)}, f32[6,128,3,128]{3,1,2,0:T(8,128)}) %tuple.56, (s32[]{:T(128)}, bf16[1280,3584]{1,0:T(8,128)(2,1)}, f32[28,128]{1,0:T(8,128)S(1)}, s32[6,3]{1,0:T(8,128)S(1)}, ...), branch_computations={%region_3.3_spmd, %region_4.4_spmd} | conditional | flops 152416256 | bytes 10107080 | solution.py:83
  88.7 4.7 gather_fusion.1
  105.3 14.7 %conditional.3 = ((f32[6,128,3,128]{3,1,2,0:T(8,128)S(1)}, f32[6,128,3,128]{3,1,2,0:T(8,128)})) conditional(s32[]{:T(128)} %convert_element_type.43, (f32[6,128,3,128]{3,1,2,0:T(8,128)S(1)}, f32[6,128,3,128]{3,1,2,0:T(8,128)}) %tuple.56, (s32[]{:T(128)}, bf16[1280,3584]{1,0:T(8,128)(2,1)}, f32[28,128]{1,0:T(8,128)S(1)}, s32[6,3]{1,0:T(8,128)S(1)}, ...), branch_computations={%region_3.3_spmd, %region_4.4_spmd} | conditional | flops 152416256 | bytes 10107080 | solution.py:83
  106.5 4.7 gather_fusion.1
  123.1 14.7 %conditional.3 = ((f32[6,128,3,128]{3,1,2,0:T(8,128)S(1)}, f32[6,128,3,128]{3,1,2,0:T(8,128)})) conditional(s32[]{:T(128)} %convert_element_type.43, (f32[6,128,3,128]{3,1,2,0:T(8,128)S(1)}, f32[6,128,3,128]{3,1,2,0:T(8,128)}) %tuple.56, (s32[]{:T(128)}, bf16[1280,3584]{1,0:T(8,128)(2,1)}, f32[28,128]{1,0:T(8,128)S(1)}, s32[6,3]{1,0:T(8,128)S(1)}, ...), branch_computations={%region_3.3_spmd, %region_4.4_spmd} | conditional | flops 152416256 | bytes 10107080 | solution.py:83
  124.3 4.7 gather_fusion.1
  140.9 14.7 %conditional.3 = ((f32[6,128,3,128]{3,1,2,0:T(8,128)S(1)}, f32[6,128,3,128]{3,1,2,0:T(8,128)})) conditional(s32[]{:T(128)} %convert_element_type.43, (f32[6,128,3,128]{3,1,2,0:T(8,128)S(1)}, f32[6,128,3,128]{3,1,2,0:T(8,128)}) %tuple.56, (s32[]{:T(128)}, bf16[1280,3584]{1,0:T(8,128)(2,1)}, f32[28,128]{1,0:T(8,128)S(1)}, s32[6,3]{1,0:T(8,128)S(1)}, ...), branch_computations={%region_3.3_spmd, %region_4.4_spmd} | conditional | flops 152416256 | bytes 10107080 | solution.py:83
  142.2 4.7 gather_fusion.1
  158.8 14.7 %conditional.3 = ((f32[6,128,3,128]{3,1,2,0:T(8,128)S(1)}, f32[6,128,3,128]{3,1,2,0:T(8,128)})) conditional(s32[]{:T(128)} %convert_element_type.43, (f32[6,128,3,128]{3,1,2,0:T(8,128)S(1)}, f32[6,128,3,128]{3,1,2,0:T(8,128)}) %tuple.56, (s32[]{:T(128)}, bf16[1280,3584]{1,0:T(8,128)(2,1)}, f32[28,128]{1,0:T(8,128)S(1)}, s32[6,3]{1,0:T(8,128)S(1)}, ...), branch_computations={%region_3.3_spmd, %region_4.4_spmd} | conditional | flops 152416256 | bytes 10107080 | solution.py:83
  160.0 4.7 gather_fusion.1
  176.6 14.7 %conditional.3 = ((f32[6,128,3,128]{3,1,2,0:T(8,128)S(1)}, f32[6,128,3,128]{3,1,2,0:T(8,128)})) conditional(s32[]{:T(128)} %convert_element_type.43, (f32[6,128,3,128]{3,1,2,0:T(8,128)S(1)}, f32[6,128,3,128]{3,1,2,0:T(8,128)}) %tuple.56, (s32[]{:T(128)}, bf16[1280,3584]{1,0:T(8,128)(2,1)}, f32[28,128]{1,0:T(8,128)S(1)}, s32[6,3]{1,0:T(8,128)S(1)}, ...), branch_computations={%region_3.3_spmd, %region_4.4_spmd} | conditional | flops 152416256 | bytes 10107080 | solution.py:83
  177.8 4.7 gather_fusion.1
  194.4 14.7 %conditional.3 = ((f32[6,128,3,128]{3,1,2,0:T(8,128)S(1)}, f32[6,128,3,128]{3,1,2,0:T(8,128)})) conditional(s32[]{:T(128)} %convert_element_type.43, (f32[6,128,3,128]{3,1,2,0:T(8,128)S(1)}, f32[6,128,3,128]{3,1,2,0:T(8,128)}) %tuple.56, (s32[]{:T(128)}, bf16[1280,3584]{1,0:T(8,128)(2,1)}, f32[28,128]{1,0:T(8,128)S(1)}, s32[6,3]{1,0:T(8,128)S(1)}, ...), branch_computations={%region_3.3_spmd, %region_4.4_spmd} | conditional | flops 152416256 | bytes 10107080 | solution.py:83
  195.6 4.7 gather_fusion.1
  212.2 14.7 %conditional.3 = ((f32[6,128,3,128]{3,1,2,0:T(8,128)S(1)}, f32[6,128,3,128]{3,1,2,0:T(8,128)})) conditional(s32[]{:T(128)} %convert_element_type.43, (f32[6,128,3,128]{3,1,2,0:T(8,128)S(1)}, f32[6,128,3,128]{3,1,2,0:T(8,128)}) %tuple.56, (s32[]{:T(128)}, bf16[1280,3584]{1,0:T(8,128)(2,1)}, f32[28,128]{1,0:T(8,128)S(1)}, s32[6,3]{1,0:T(8,128)S(1)}, ...), branch_computations={%region_3.3_spmd, %region_4.4_spmd} | conditional | flops 152416256 | bytes 10107080 | solution.py:83
  213.5 4.7 gather_fusion.1
  230.0 14.7 %conditional.3 = ((f32[6,128,3,128]{3,1,2,0:T(8,128)S(1)}, f32[6,128,3,128]{3,1,2,0:T(8,128)})) conditional(s32[]{:T(128)} %convert_element_type.43, (f32[6,128,3,128]{3,1,2,0:T(8,128)S(1)}, f32[6,128,3,128]{3,1,2,0:T(8,128)}) %tuple.56, (s32[]{:T(128)}, bf16[1280,3584]{1,0:T(8,128)(2,1)}, f32[28,128]{1,0:T(8,128)S(1)}, s32[6,3]{1,0:T(8,128)S(1)}, ...), branch_computations={%region_3.3_spmd, %region_4.4_spmd} | conditional | flops 152416256 | bytes 10107080 | solution.py:83
  247.9 14.7 %conditional.3 = ((f32[6,128,3,128]{3,1,2,0:T(8,128)S(1)}, f32[6,128,3,128]{3,1,2,0:T(8,128)})) conditional(s32[]{:T(128)} %convert_element_type.43, (f32[6,128,3,128]{3,1,2,0:T(8,128)S(1)}, f32[6,128,3,128]{3,1,2,0:T(8,128)}) %tuple.56, (s32[]{:T(128)}, bf16[1280,3584]{1,0:T(8,128)(2,1)}, f32[28,128]{1,0:T(8,128)S(1)}, s32[6,3]{1,0:T(8,128)S(1)}, ...), branch_computations={%region_3.3_spmd, %region_4.4_spmd} | conditional | flops 152416256 | bytes 10107080 | solution.py:83
  265.7 14.7 %conditional.3 = ((f32[6,128,3,128]{3,1,2,0:T(8,128)S(1)}, f32[6,128,3,128]{3,1,2,0:T(8,128)})) conditional(s32[]{:T(128)} %convert_element_type.43, (f32[6,128,3,128]{3,1,2,0:T(8,128)S(1)}, f32[6,128,3,128]{3,1,2,0:T(8,128)}) %tuple.56, (s32[]{:T(128)}, bf16[1280,3584]{1,0:T(8,128)(2,1)}, f32[28,128]{1,0:T(8,128)S(1)}, s32[6,3]{1,0:T(8,128)S(1)}, ...), branch_computations={%region_3.3_spmd, %region_4.4_spmd} | conditional | flops 152416256 | bytes 10107080 | solution.py:83
  289.8 14.7 %conditional.3 = ((f32[6,128,3,128]{3,1,2,0:T(8,128)S(1)}, f32[6,128,3,128]{3,1,2,0:T(8,128)})) conditional(s32[]{:T(128)} %convert_element_type.43, (f32[6,128,3,128]{3,1,2,0:T(8,128)S(1)}, f32[6,128,3,128]{3,1,2,0:T(8,128)}) %tuple.56, (s32[]{:T(128)}, bf16[1280,3584]{1,0:T(8,128)(2,1)}, f32[28,128]{1,0:T(8,128)S(1)}, s32[6,3]{1,0:T(8,128)S(1)}, ...), branch_computations={%region_3.3_spmd, %region_4.4_spmd} | conditional | flops 152416256 | bytes 10107080 | solution.py:83
  307.6 14.7 %conditional.3 = ((f32[6,128,3,128]{3,1,2,0:T(8,128)S(1)}, f32[6,128,3,128]{3,1,2,0:T(8,128)})) conditional(s32[]{:T(128)} %convert_element_type.43, (f32[6,128,3,128]{3,1,2,0:T(8,128)S(1)}, f32[6,128,3,128]{3,1,2,0:T(8,128)}) %tuple.56, (s32[]{:T(128)}, bf16[1280,3584]{1,0:T(8,128)(2,1)}, f32[28,128]{1,0:T(8,128)S(1)}, s32[6,3]{1,0:T(8,128)S(1)}, ...), branch_computations={%region_3.3_spmd, %region_4.4_spmd} | conditional | flops 152416256 | bytes 10107080 | solution.py:83
  325.4 14.7 %conditional.3 = ((f32[6,128,3,128]{3,1,2,0:T(8,128)S(1)}, f32[6,128,3,128]{3,1,2,0:T(8,128)})) conditional(s32[]{:T(128)} %convert_element_type.43, (f32[6,128,3,128]{3,1,2,0:T(8,128)S(1)}, f32[6,128,3,128]{3,1,2,0:T(8,128)}) %tuple.56, (s32[]{:T(128)}, bf16[1280,3584]{1,0:T(8,128)(2,1)}, f32[28,128]{1,0:T(8,128)S(1)}, s32[6,3]{1,0:T(8,128)S(1)}, ...), branch_computations={%region_3.3_spmd, %region_4.4_spmd} | conditional | flops 152416256 | bytes 10107080 | solution.py:83
  343.2 14.7 %conditional.3 = ((f32[6,128,3,128]{3,1,2,0:T(8,128)S(1)}, f32[6,128,3,128]{3,1,2,0:T(8,128)})) conditional(s32[]{:T(128)} %convert_element_type.43, (f32[6,128,3,128]{3,1,2,0:T(8,128)S(1)}, f32[6,128,3,128]{3,1,2,0:T(8,128)}) %tuple.56, (s32[]{:T(128)}, bf16[1280,3584]{1,0:T(8,128)(2,1)}, f32[28,128]{1,0:T(8,128)S(1)}, s32[6,3]{1,0:T(8,128)S(1)}, ...), branch_computations={%region_3.3_spmd, %region_4.4_spmd} | conditional | flops 152416256 | bytes 10107080 | solution.py:83
  344.5 4.7 gather_fusion.1
  361.1 14.7 %conditional.3 = ((f32[6,128,3,128]{3,1,2,0:T(8,128)S(1)}, f32[6,128,3,128]{3,1,2,0:T(8,128)})) conditional(s32[]{:T(128)} %convert_element_type.43, (f32[6,128,3,128]{3,1,2,0:T(8,128)S(1)}, f32[6,128,3,128]{3,1,2,0:T(8,128)}) %tuple.56, (s32[]{:T(128)}, bf16[1280,3584]{1,0:T(8,128)(2,1)}, f32[28,128]{1,0:T(8,128)S(1)}, s32[6,3]{1,0:T(8,128)S(1)}, ...), branch_computations={%region_3.3_spmd, %region_4.4_spmd} | conditional | flops 152416256 | bytes 10107080 | solution.py:83
  378.9 14.7 %conditional.3 = ((f32[6,128,3,128]{3,1,2,0:T(8,128)S(1)}, f32[6,128,3,128]{3,1,2,0:T(8,128)})) conditional(s32[]{:T(128)} %convert_element_type.43, (f32[6,128,3,128]{3,1,2,0:T(8,128)S(1)}, f32[6,128,3,128]{3,1,2,0:T(8,128)}) %tuple.56, (s32[]{:T(128)}, bf16[1280,3584]{1,0:T(8,128)(2,1)}, f32[28,128]{1,0:T(8,128)S(1)}, s32[6,3]{1,0:T(8,128)S(1)}, ...), branch_computations={%region_3.3_spmd, %region_4.4_spmd} | conditional | flops 152416256 | bytes 10107080 | solution.py:83
  425.6 425.7 %all-reduce.5.cloned.1.call-done = (f32[768,384]{0,1:T(8,128)}, f32[768,384]{0,1:T(8,128)}) async-done(((f32[768,384]{0,1:T(8,128)}, f32[768,384]{0,1:T(8,128)}), (f32[768,384]{0,1:T(8,128)}, f32[768,384]{0,1:T(8,128)})) %all-reduce.5.cloned.1.call-update) | async-done | bytes 2359312
  (305 shorter events, 281.9 us)
Async XLA Ops:
  7.2 9.6 %copy-start.3 = (s32[2]{0:T(128)S(1)}, s32[2]{0:T(128)}, u32[]{:S(2)}) copy-start(s32[2]{0:T(128)} %param.13) | copy-start | bytes 28
  7.2 11.8 %copy-start.2 = (s32[6,3]{0,1:T(4,128)S(1)}, s32[6,3]{0,1:T(4,128)}, u32[]{:S(2)}) copy-start(s32[6,3]{0,1:T(4,128)} %param.15) | copy-start | bytes 220
  7.2 11.8 %copy-start.4 = (s32[2]{0:T(128)S(1)}, s32[2]{0:T(128)}, u32[]{:S(2)}) copy-start(s32[2]{0:T(128)} %param.14) | copy-start | bytes 28
  7.2 17.1 %copy-start = (f32[3584]{0:T(1024)S(1)}, f32[3584]{0:T(1024)}, u32[]{:S(2)}) copy-start(f32[3584]{0:T(1024)} %param.11) | copy-start | bytes 43012
  7.2 17.1 %copy-start.1 = (f32[3584]{0:T(1024)S(1)}, f32[3584]{0:T(1024)}, u32[]{:S(2)}) copy-start(f32[3584]{0:T(1024)} %param.12) | copy-start | bytes 43012
  7.2 844.1 %all-reduce.5.cloned.1.call-start = ((), (), s32[]{:S(2)}) async-start(), calls=%async_computation | async-start | bytes 4718592
  11.3 43.0 %collective-permute-start = (bf16[256,3584]{1,0:T(8,128)(2,1)}, bf16[256,3584]{1,0:T(8,128)(2,1)S(1)}, u32[]{:S(2)}, u32[]{:S(2)}) collective-permute-start(bf16[256,3584]{1,0:T(8,128)(2,1)} %get-tuple-element.265), channel_id=1, source_target_pairs={{0,1},{1,2},{2,3},{3,4},{4,5},{5,6},{6,7},{8,9},{9,10},{10,11},{11... | collective-permute-start | bytes 5505032 | tf_op jit(solution)/shard_map/ppermute | solution.py:18
  15.5 42.8 %collective-permute-start.1 = (bf16[256,3584]{1,0:T(8,128)(2,1)}, bf16[256,3584]{1,0:T(8,128)(2,1)}, u32[]{:S(2)}, u32[]{:S(2)}) collective-permute-start(bf16[256,3584]{1,0:T(8,128)(2,1)} %get-tuple-element.266), channel_id=1, source_target_pairs={{1,0},{2,1},{3,2},{4,3},{5,4},{6,5},{7,6},{9,8},{10,9},{11,10},{12... | collective-permute-start | bytes 5505032 | tf_op jit(solution)/shard_map/ppermute | solution.py:19
  423.7 0.7 copy-start.5
Sparse Core Ops, SparseCore 0:
  423.8 427.4 all-reduce.4
where the time goes:
time: 866 us; the launch traced here: 862 us
  waiting for transfers between devices  460 us (53%)
  local copies, waits for them, and re-layouts  235 us (27%)
  matrix products  56.7 us (7%)
  loops' own time  55.7 us (6%)
  other arithmetic  34.3 us (4%)
  between operations  14.8 us (2%)
    unnamed x2, waiting for transfers between devices  426 us
    gather x18, local copies, waits for them, and re-layouts, add_terms(): far_panel_e = scaled_e[row_index]  84.1 us
    gather x18, local copies, waits for them, and re-layouts, add_terms(): far_panel = scaled[row_index]  83.9 us
    another operation x1, loops' own time, shards(): totals = lax.fori_loop(0, panels, add_own, (zeros, zeros))  54.3 us
    dot_general x18, matrix products, add_terms(): jnp.einsum('bik,bjck->bijc', own_three, far_panel_e, preferred_element_ty...  48.1 us
    ppermute x1, waiting for transfers between devices, with_halo(): before = lax.ppermute(last, axis, up)  30 us
    convert_element_type x18, other arithmetic, add_terms(): scaled_e = (wide * we_panel[None, :]).astype(jnp.bfloat16)  19.6 us
  transfers between devices with their start and end apart: 3, of which 3 were waited for; matrix products, arithmetic and copies ran while one was open for 1% of the time, Pallas kernels for 0%

commit v1 on v0

v1 whole, which is shorter than its diff:
```python
import functools

import jax
import jax.numpy as jnp
from jax import lax
from jax.experimental import pallas as pl
from jax.experimental.pallas import tpu as pltpu
from jax.sharding import PartitionSpec as P

BS = 128
COLS = 1792
CHUNK = 512
MESH = pl.DeviceIdType.MESH
F32, BF16 = jnp.float32, jnp.bfloat16


def dot_t(a, b):
    return lax.dot_general(a, b, (((1,), (1,)), ((), ())), preferred_element_type=F32)


def kernel(
    nband, nz, cols_per_slice, chunk,
    eig, energies, smearing, counts, occupied, block_cols, dens, edens,
    e, halo, w, we, q, cross_a, cross_b,
    stage, pair_in, zsend, zrecv, xsum, xrecv,
    lstage, lpair_in, lsend, larecv, lbrecv, lxsum, lxrecv, late,
    load_sem, halo_ss, halo_rs, pair_ss, pair_rs, z_ss, z_rs, x_ss, x_rs,
    lpair_ss, lpair_rs, la_ss, la_rs, lb_ss, lb_rs, lx_ss, lx_rs,
):
    rows, cols = eig.shape
    nk = cols // chunk
    nblk = rows // BS
    own = dens.shape[0]
    rz = rows // nz
    low = -(-2 * BS // rz)
    high = nz - (rows - 2 * BS) // rz
    blow = -(-BS // rz)
    bhigh = nz - (rows - BS) // rz
    a_z = list(range(low)) + list(range(nz - high, nz))
    na = len(a_z)
    up_z = list(range(blow))
    dn_z = list(range(nz - bhigh, nz))

    me = lax.axis_index("cuts")
    band = lax.axis_index("band")
    z, xh, core = me // 4, me // 2 % 2, me % 2
    nxt, prv = (band + 1) % nband, (band + nband - 1) % nband
    lane = xh * 2 + core

    def dev(b, zz, x=None, c=None):
        return {"cuts": zz * 4 + (xh if x is None else x) * 2 + (core if c is None else c), "band": b}

    barrier = pltpu.get_barrier_semaphore()

    def greet(device):
        pl.semaphore_signal(barrier, inc=1, device_id=device, device_id_type=MESH)

    greet(dev(nxt, z))
    greet(dev(prv, z))
    greet(dev(band, z, c=1 - core))
    greet(dev(band, z, x=1 - xh))
    for k in range(1, nz):
        greet(dev(band, (z + k) % nz))

    @pl.when(z < blow)
    def _():
        for k in range(nz):
            greet(dev(prv, k))

    @pl.when(z >= nz - bhigh)
    def _():
        for k in range(nz):
            greet(dev(nxt, k))

    loads = []
    for k in range(nk):
        load = pltpu.make_async_copy(eig.at[:, pl.ds(k * chunk, chunk)], e.at[k], load_sem.at[k])
        load.start()
        loads.append(load)

    pl.semaphore_wait(barrier, 4 + (nz - 1) + blow + bhigh)

    def halo_copy(side, k):
        first = 0 if side == 0 else rows - BS
        start = k * chunk if isinstance(k, int) else pl.multiple_of(k * chunk, 128)
        return pltpu.make_async_remote_copy(
            src_ref=eig.at[pl.ds(first, BS), pl.ds(start, chunk)],
            dst_ref=halo.at[side, k],
            send_sem=halo_ss.at[side, k],
            recv_sem=halo_rs.at[side, k],
            device_id=dev(prv if side == 0 else nxt, z),
            device_id_type=MESH,
        )

    for k in range(nk):
        halo_copy(0, k).start()
        halo_copy(1, k).start()

    slot = lax.broadcasted_iota(jnp.int32, (1, cols), 1)
    weight = jnp.zeros((1, cols), F32)
    for s in range(cols // cols_per_slice):
        within = slot - s * cols_per_slice
        live = (within >= 0) & (within < counts[s])
        weight = jnp.where(live, jnp.where(within < occupied[s], 2.0, smearing[...]), weight)
    w[...] = weight
    we[...] = weight * energies[...]

    def scaled(block, k):
        at = pl.ds(pl.multiple_of(k * chunk, 128), chunk)
        wide = block.astype(F32)
        return jnp.concatenate(
            [(wide * w[:, at]).astype(BF16), (wide * we[:, at]).astype(BF16)], axis=0
        )

    q[...] = jnp.zeros_like(q)
    cross_a[...] = jnp.zeros_like(cross_a)
    cross_b[...] = jnp.zeros_like(cross_b)
    lstage[...] = jnp.zeros_like(lstage)
    late[...] = jnp.zeros_like(late)

    def inner(k, carry):
        pltpu.make_async_copy(
            eig.at[:, pl.ds(pl.multiple_of(k * chunk, 128), chunk)], e.at[k], load_sem.at[k]
        ).wait()
        for j in range(nblk):
            lo, hi = max(j - 2, 0), min(j + 3, nblk)
            got = dot_t(e[k, lo * BS : hi * BS, :], scaled(e[k, j * BS : (j + 1) * BS, :], k))
            for i in range(lo, hi):
                q[i * 5 + j - i + 2] += got[(i - lo) * BS : (i - lo + 1) * BS]
        return carry

    lax.fori_loop(0, nk, inner, 0)

    def place(target, block, row0, lanes):
        for o in range(row0 // own, -(-(row0 + BS) // own)):
            lo, hi = max(row0, own * o), min(row0 + BS, own * (o + 1))
            part = block[lo - row0 : hi - row0]
            at = (o % 2, o // 4, o // 2 % 2)
            target[at + (slice(lo - own * o, hi - own * o), lanes)] = part[:, :BS]
            target[at + (slice(own + lo - own * o, own + hi - own * o), lanes)] = part[:, BS:]

    first_block = band * nblk
    for i in range(nblk):
        for j in range(3):
            d = 2 if j == 0 else jnp.clip(block_cols[i, j] - first_block - i + 2, 0, 4)
            place(stage, q[i * 5 + d], i * BS, slice(j * BS, (j + 1) * BS))

    pair = pltpu.make_async_remote_copy(
        src_ref=stage.at[1 - core], dst_ref=pair_in, send_sem=pair_ss, recv_sem=pair_rs,
        device_id=dev(band, z, c=1 - core), device_id_type=MESH,
    )
    pair.start()

    def outer(k, carry):
        halo_copy(0, k).wait_recv()
        halo_copy(1, k).wait_recv()
        ahead, behind = halo[0, k], halo[1, k]
        cross_a[0] += dot_t(e[k, rows - 2 * BS :, :], scaled(ahead, k))
        cross_b[0] += dot_t(ahead, scaled(e[k, rows - 2 * BS : rows - BS, :], k))
        cross_a[1] += dot_t(e[k, : 2 * BS, :], scaled(behind, k))
        cross_b[1] += dot_t(behind, scaled(e[k, BS : 2 * BS, :], k))
        return carry

    first_cut, second_cut = max(nk * 2 // 7, 1), max(nk * 6 // 7, 1)
    lax.fori_loop(0, first_cut, outer, 0)

    pair.wait_recv()
    for t in range(nz):
        zsend[t] = (stage[core, t] + pair_in[t]).astype(BF16)

    def z_copy(k):
        there = (z + k) % nz
        return pltpu.make_async_remote_copy(
            src_ref=zsend.at[there], dst_ref=zrecv.at[k], send_sem=z_ss.at[k], recv_sem=z_rs.at[k],
            device_id=dev(band, there), device_id_type=MESH,
        )

    for k in range(1, nz):
        z_copy(k).start()

    lax.fori_loop(first_cut, second_cut, outer, 0)

    total = stage[core, z] + pair_in[z]
    for k in range(1, nz):
        z_copy(k).wait_recv()
        total = total + zrecv[k].astype(F32)
    xsum[...] = total
    x_copy = pltpu.make_async_remote_copy(
        src_ref=xsum.at[1 - xh], dst_ref=xrecv, send_sem=x_ss, recv_sem=x_rs,
        device_id=dev(band, z, x=1 - xh), device_id_type=MESH,
    )
    x_copy.start()

    lax.fori_loop(second_cut, nk, outer, 0)

    for s, zz in enumerate(a_z):
        for o in range(4 * zz, 4 * zz + 4):
            for side, base in ((1, 0), (0, rows - 2 * BS)):
                lo, hi = max(base, own * o), min(base + 2 * BS, own * (o + 1))
                if lo < hi:
                    at = (o % 2, s, o // 2 % 2)
                    lstage[at + (slice(lo - own * o, hi - own * o),)] = cross_a[side, lo - base : hi - base, :BS]
                    lstage[at + (slice(own + lo - own * o, own + hi - own * o),)] = cross_a[side, lo - base : hi - base, BS:]
    for s, (zz, side, base) in enumerate([(t, 0, 0) for t in up_z] + [(t, 1, rows - BS) for t in dn_z]):
        for o in range(4 * zz, 4 * zz + 4):
            lo, hi = max(base, own * o), min(base + BS, own * (o + 1))
            if lo < hi:
                at = (o % 2, na + s, o // 2 % 2)
                lstage[at + (slice(lo - own * o, hi - own * o),)] = cross_b[side, lo - base : hi - base, :BS]
                lstage[at + (slice(own + lo - own * o, own + hi - own * o),)] = cross_b[side, lo - base : hi - base, BS:]

    lpair = pltpu.make_async_remote_copy(
        src_ref=lstage.at[1 - core], dst_ref=lpair_in, send_sem=lpair_ss, recv_sem=lpair_rs,
        device_id=dev(band, z, c=1 - core), device_id_type=MESH,
    )
    lpair.start()
    lpair.wait_recv()
    lsend[...] = (lstage[core] + lpair_in[...]).astype(BF16)

    def a_copy(s, zz, origin):
        return pltpu.make_async_remote_copy(
            src_ref=lsend.at[s], dst_ref=larecv.at[origin], send_sem=la_ss.at[s], recv_sem=la_rs.at[origin],
            device_id=dev(band, zz), device_id_type=MESH,
        )

    def b_copy(s, b, zz, origin):
        return pltpu.make_async_remote_copy(
            src_ref=lsend.at[na + s], dst_ref=lbrecv.at[origin], send_sem=lb_ss.at[s], recv_sem=lb_rs.at[origin],
            device_id=dev(b, zz), device_id_type=MESH,
        )

    b_list = [(s, nxt, zz) for s, zz in enumerate(up_z)]
    b_list += [(blow + s, prv, zz) for s, zz in enumerate(dn_z)]
    for s, b, zz in b_list:
        b_copy(s, b, zz, z).start()
    for s, zz in enumerate(a_z):
        pl.when(z != zz)(a_copy(s, zz, z).start)

    is_a = (z < low) | (z >= nz - high)
    is_b = (z < blow) | (z >= nz - bhigh)

    lx = pltpu.make_async_remote_copy(
        src_ref=lxsum.at[1 - xh], dst_ref=lxrecv, send_sem=lx_ss, recv_sem=lx_rs,
        device_id=dev(band, z, x=1 - xh), device_id_type=MESH,
    )

    @pl.when(is_a)
    def _():
        mine = jnp.where(z < low, z, z - (nz - na))
        sum_a = lstage[core, mine] + lpair_in[mine]
        for k in range(1, nz):
            origin = (z + k) % nz
            a_copy(0, 0, origin).wait_recv()
            sum_a = sum_a + larecv[origin].astype(F32)
        lxsum[:, 0] = sum_a
        lxsum[:, 1] = jnp.zeros_like(sum_a)

        @pl.when(is_b)
        def _():
            sum_b = jnp.zeros_like(sum_a)
            for k in range(nz):
                b_copy(0, nxt, 0, k).wait_recv()
                sum_b = sum_b + lbrecv[k].astype(F32)
            lxsum[:, 1] = sum_b

        lx.start()
        lx.wait_recv()
        late[...] = lxsum[xh] + lxrecv[...]

    x_copy.wait_recv()
    early = xsum[xh] + xrecv[...]
    row_block = (lax.broadcasted_iota(jnp.int32, (own, BS), 0) + own * me) // BS
    for j in range(3):
        for out, start in ((dens, 0), (edens, own)):
            value = early[start : start + own, j * BS : (j + 1) * BS]
            if j:
                for part, wanted in (
                    (0, ((0, -1), (1, -1), (nblk - 2, nblk), (nblk - 1, nblk))),
                    (1, ((0, -2), (nblk - 1, nblk + 1))),
                ):
                    mask = None
                    for i, rel in wanted:
                        hit = jnp.where(block_cols[i, j] - first_block == rel, i, -1)
                        mask = (row_block == hit) if mask is None else mask | (row_block == hit)
                    value = value + jnp.where(mask, late[part, start : start + own, :], 0.0)
            out[:, j * BS : (j + 1) * BS] = value

    for k in range(nk):
        halo_copy(0, k).wait_send()
        halo_copy(1, k).wait_send()
    pair.wait_send()
    for k in range(1, nz):
        z_copy(k).wait_send()
    x_copy.wait_send()
    lpair.wait_send()
    for s, b, zz in b_list:
        b_copy(s, b, zz, z).wait_send()
    for s, zz in enumerate(a_z):
        pl.when(z != zz)(a_copy(s, zz, z).wait_send)
    pl.when(is_a)(lx.wait_send)


def shards(nband, nz, cols_per_slice, chunk, eigvecs, energies, smearing, counts, occupied, block_cols):
    rows, cols = eigvecs.shape
    nk = cols // chunk
    nblk = rows // BS
    own = rows // (nz * 4)
    rz = rows // nz
    na = -(-2 * BS // rz) + nz - (rows - 2 * BS) // rz
    nb = -(-BS // rz) + nz - (rows - BS) // rz
    vmem = pl.BlockSpec(memory_space=pltpu.VMEM)
    smem = pl.BlockSpec(memory_space=pltpu.SMEM)
    dma = pltpu.SemaphoreType.DMA
    wide = 3 * BS
    return pl.pallas_call(
        functools.partial(kernel, nband, nz, cols_per_slice, chunk),
        out_shape=(jax.ShapeDtypeStruct((own, wide), F32),) * 2,
        in_specs=[pl.BlockSpec(memory_space=pl.ANY), vmem, vmem, smem, smem, smem],
        out_specs=(vmem, vmem),
        scratch_shapes=[
            pltpu.VMEM((nk, rows, chunk), BF16),
            pltpu.VMEM((2, nk, BS, chunk), BF16),
            pltpu.VMEM((1, cols), F32),
            pltpu.VMEM((1, cols), F32),
            pltpu.VMEM((nblk * 5, BS, 2 * BS), F32),
            pltpu.VMEM((2, 2 * BS, 2 * BS), F32),
            pltpu.VMEM((2, BS, 2 * BS), F32),
            pltpu.VMEM((2, nz, 2, 2 * own, wide), F32),
            pltpu.VMEM((nz, 2, 2 * own, wide), F32),
            pltpu.VMEM((nz, 2, 2 * own, wide), BF16),
            pltpu.VMEM((nz, 2, 2 * own, wide), BF16),
            pltpu.VMEM((2, 2 * own, wide), F32),
            pltpu.VMEM((2 * own, wide), F32),
            pltpu.VMEM((2, na + nb, 2, 2 * own, BS), F32),
            pltpu.VMEM((na + nb, 2, 2 * own, BS), F32),
            pltpu.VMEM((na + nb, 2, 2 * own, BS), BF16),
            pltpu.VMEM((nz, 2, 2 * own, BS), BF16),
            pltpu.VMEM((nz, 2, 2 * own, BS), BF16),
            pltpu.VMEM((2, 2, 2 * own, BS), F32),
            pltpu.VMEM((2, 2 * own, BS), F32),
            pltpu.VMEM((2, 2 * own, BS), F32),
            dma((nk,)), dma((2, nk)), dma((2, nk)), dma, dma, dma((nz,)), dma((nz,)), dma, dma,
            dma, dma, dma((na,)), dma((nz,)), dma((nb,)), dma((nz,)), dma, dma,
        ],
        compiler_params=pltpu.CompilerParams(
            collective_id=0, has_side_effects=True, vmem_limit_bytes=48 * 1024 * 1024
        ),
        cost_estimate=pl.CostEstimate(
            flops=2 * 48 * BS * BS * cols, bytes_accessed=rows * cols * 2, transcendentals=0
        ),
    )(eigvecs, energies.reshape(1, cols), smearing.reshape(1, cols), counts, occupied, block_cols)


def build(mesh, cols_per_slice, chunk):
    placed = (P("band", "cuts"), P("cuts"), P("cuts"), P("cuts"), P("cuts"), P("band", None))
    body = functools.partial(shards, mesh.shape["band"], mesh.shape["cuts"] // 4, cols_per_slice, chunk)
    return jax.shard_map(
        body,
        mesh=mesh,
        in_specs=placed,
        out_specs=(P(("band", "cuts"), None), P(("band", "cuts"), None)),
        check_vma=False,
    )


def solution(mesh):
    return build(mesh, COLS, CHUNK)
```

time: 866 us -> 62.6 us (0.07)
  waiting for transfers between devices: 460 us -> 0 us
  local copies, waits for them, and re-layouts: 235 us -> 7.33 us
  matrix products: 56.7 us -> 0 us
  loops' own time: 55.7 us -> 0 us
  Pallas kernels: 0 us -> 54.4 us
  other arithmetic: 34.3 us -> 0 us
  between operations: 14.8 us -> 0.66 us
    unnamed x2 -> x0, waiting for transfers between devices: 426 us -> none
    gather x38 -> x0, local copies, waits for them, and re-layouts: 169 us -> none  [the longest x18 84.1 us: add_terms(): far_panel_e = scaled_e[row_index]]
    dot_general x36 -> x0, matrix products: 56.7 us -> none  [the longest x18 48.1 us: add_terms(): jnp.einsum('bik,bjck->bijc', own_three, far_panel_e, preferred_element_ty...]
    another operation x29 -> x0, loops' own time: 55.7 us -> none  [the longest x1 54.3 us: shards(): totals = lax.fori_loop(0, panels, add_own, (zeros, zeros))]
    pallas_call x0 -> x1, Pallas kernels: none -> 54.4 us  [shards(): pl.pallas_call(functools.partial(kernel, nband, nz, cols_per_slice, chunk...]
    dynamic_slice x74 -> x0, local copies, waits for them, and re-layouts: 50.1 us -> none  [the longest x18 17.1 us: add_terms(): own_panel = lax.dynamic_slice_in_dim(pad_panel, 2 * BS, rows, 0)]
    ppermute x2 -> x0, waiting for transfers between devices: 34 us -> none  [the longest x1 30 us: with_halo(): before = lax.ppermute(last, axis, up)]
    convert_element_type x19 -> x0, other arithmetic: 20.9 us -> none  [the longest x18 19.6 us: add_terms(): scaled_e = (wide * we_panel[None, :]).astype(jnp.bfloat16)]
  transfers between devices with their start and end apart: 3 -> 0, of which waited for: 3 -> 0; matrix products, arithmetic and copies ran while one was open for 1% -> 0% of each run, Pallas kernels for 0% -> 0%
where the time goes in v1:
time: 62.6 us; the launch traced here: 62.3 us
  Pallas kernels  54.4 us (87%)
  local copies, waits for them, and re-layouts  7.33 us (12%)
  between operations  0.66 us (1%)
    pallas_call x1, Pallas kernels, shards(): pl.pallas_call(functools.partial(kernel, nband, nz, cols_per_slice, chunk...  54.4 us
    unnamed x9, local copies, waits for them, and re-layouts  5.87 us

profile of v1, /device:TPU:1, one launch (start us, length us, event | category | flops | bytes accessed | tf_op | source)
XLA Modules:
  0.0 62.3 jit_solution(11270060644128399372)
XLA Ops:
  0.6 0.8 %copy.8.block_cols = s32[6,3]{1,0:T(8,128)S(1)} copy(s32[6,3]{0,1:T(4,128)} %param.11) | data formatting | bytes 144 | tf_op args[5]
  1.4 0.7 %reshape.10.energies = f32[1,3584]{1,0:T(1,128)S(1)} reshape(f32[3584]{0:T(1024)} %param.7) | data formatting | bytes 28672 | tf_op jit(solution)/shard_map/reshape | solution.py:351
  2.1 0.7 %reshape.11.smearing = f32[1,3584]{1,0:T(1,128)S(1)} reshape(f32[3584]{0:T(1024)} %param.8) | data formatting | bytes 28672 | tf_op jit(solution)/shard_map/reshape | solution.py:351
  2.9 0.0 copy-start
  2.9 2.6 %copy-done = bf16[768,3584]{1,0:T(8,128)(2,1)S(1)} copy-done((bf16[768,3584]{1,0:T(8,128)(2,1)S(1)}, bf16[768,3584]{1,0:T(8,128)(2,1)}, u32[]{:S(2)}) %copy-start) | copy-done | bytes 5505048
  5.4 0.0 copy-start.1
  5.4 0.7 %copy-done.1 = s32[2]{0:T(128)S(1)} copy-done((s32[2]{0:T(128)S(1)}, s32[2]{0:T(128)}, u32[]{:S(2)}) %copy-start.1) | copy-done | bytes 32
  6.1 0.0 copy-start.2
  6.1 0.7 %copy-done.2 = s32[2]{0:T(128)S(1)} copy-done((s32[2]{0:T(128)S(1)}, s32[2]{0:T(128)}, u32[]{:S(2)}) %copy-start.2) | copy-done | bytes 32
  6.7 54.4 %shard_map.77 = (f32[24,384]{1,0:T(8,128)S(1)}, f32[24,384]{1,0:T(8,128)S(1)}) custom-call(bf16[768,3584]{1,0:T(8,128)(2,1)S(1)} %copy-done, f32[1,3584]{1,0:T(1,128)S(1)} %reshape.10.energies, f32[1,3584]{1,0:T(1,128)S(1)} %reshape.11.smearing, s32[2]{0:T(128)S(1)} %copy-done.1, s32[2]{0:T(128)S(1)} %copy-done.2, s32[6,3]{1,0:T(8,128)S(1)} %copy.8.block_cols), custom_call_target="tpu_custom_call" | custom-call | flops 5637144576 | bytes 5505024 | tf_op jit(solution)/shard_map/pallas_call | solution.py:315
  61.1 0.6 copy.11
  61.7 0.6 copy.12
Async XLA Ops:
  2.9 2.6 %copy-start = (bf16[768,3584]{1,0:T(8,128)(2,1)S(1)}, bf16[768,3584]{1,0:T(8,128)(2,1)}, u32[]{:S(2)}) copy-start(bf16[768,3584]{1,0:T(8,128)(2,1)} %eig.1) | copy-start | bytes 16515076
  5.4 0.7 %copy-start.1 = (s32[2]{0:T(128)S(1)}, s32[2]{0:T(128)}, u32[]{:S(2)}) copy-start(s32[2]{0:T(128)} %counts.1) | copy-start | bytes 28
  6.1 0.7 %copy-start.2 = (s32[2]{0:T(128)S(1)}, s32[2]{0:T(128)}, u32[]{:S(2)}) copy-start(s32[2]{0:T(128)} %occupied.1) | copy-start | bytes 28

commit v2 on v1

v2 whole, which is shorter than its diff:
```python
import functools

import jax
import jax.numpy as jnp
from jax import lax
from jax.experimental import pallas as pl
from jax.experimental.pallas import tpu as pltpu
from jax.sharding import PartitionSpec as P

BS = 128
COLS = 1792
CHUNK = 512
HALF = BS // 2
VMEM_LIMIT = 60 * 1024 * 1024
MESH = pl.DeviceIdType.MESH
F32, BF16 = jnp.float32, jnp.bfloat16


def dot_t(a, b):
    return lax.dot_general(a, b, (((1,), (1,)), ((), ())), preferred_element_type=F32)


def kernel(
    nband, nz, cols_per_slice, chunk,
    eig, energies_in, smearing_in, counts_in, occupied_in, cols_in, dens, edens,
    energies, smearing, counts, occupied, block_cols, e, halo, w, we, sb, q, cross_a, cross_b,
    stage, pair_in, rsend, rrecv, xsum, xrecv,
    lstage, lpair_in, lsend, larecv, lbrecv, lxsum, lxrecv, late,
    small_sem, load_sem, halo_ss, halo_rs, pair_ss, pair_rs, r_ss, r_rs, x_ss, x_rs,
    lpair_ss, lpair_rs, la_ss, la_rs, lb_ss, lb_rs, lx_ss, lx_rs,
):
    rows, cols = eig.shape
    nk = cols // chunk
    nblk = rows // BS
    own = dens.shape[0]
    rz = rows // nz
    steps = nz // 2
    a_z = outer_z(rows, nz)
    na = len(a_z)
    low = na // 2
    b_z = [boundary_z(rows, nz, p) for p in range(2)]
    up_all = sorted(set(b_z[0][0] + b_z[1][0]))
    dn_all = sorted(set(b_z[0][1] + b_z[1][1]))

    me = lax.axis_index("cuts")
    band = lax.axis_index("band")
    z, xh, core = me // 4, me // 2 % 2, me % 2
    nxt, prv = (band + 1) % nband, (band + nband - 1) % nband

    def dev(b, zz, x=None, c=None):
        return {"cuts": zz * 4 + (xh if x is None else x) * 2 + (core if c is None else c), "band": b}

    def remote(src, dst, send_sem, recv_sem, device):
        return pltpu.make_async_remote_copy(
            src_ref=src, dst_ref=dst, send_sem=send_sem, recv_sem=recv_sem,
            device_id=device, device_id_type=MESH,
        )

    barrier = pltpu.get_barrier_semaphore()

    def greet(device):
        pl.semaphore_signal(barrier, inc=1, device_id=device, device_id_type=MESH)

    greet(dev(nxt, z))
    greet(dev(prv, z))
    greet(dev(band, z, c=1 - core))
    greet(dev(band, z, x=1 - xh))
    for k in range(1, nz):
        greet(dev(band, (z + k) % nz))

    @pl.when(z < len(up_all))
    def _():
        for k in range(nz):
            greet(dev(prv, k))

    @pl.when(z >= nz - len(dn_all))
    def _():
        for k in range(nz):
            greet(dev(nxt, k))

    smalls = []
    for t, (src, dst) in enumerate((
        (energies_in, energies), (smearing_in, smearing),
        (counts_in, counts), (occupied_in, occupied), (cols_in, block_cols),
    )):
        small = pltpu.make_async_copy(src, dst, small_sem.at[t])
        small.start()
        smalls.append(small)
    for k in range(nk):
        pltpu.make_async_copy(eig.at[:, pl.ds(k * chunk, chunk)], e.at[k], load_sem.at[k]).start()

    pl.semaphore_wait(barrier, 4 + (nz - 1) + len(up_all) + len(dn_all))

    def halo_copy(p, side, k):
        first = HALF * (1 - p) if side == 0 else rows - BS + HALF * p
        start = k * chunk if isinstance(k, int) else pl.multiple_of(k * chunk, 128)
        return remote(
            eig.at[pl.ds(first, HALF), pl.ds(start, chunk)], halo.at[p, side, k],
            halo_ss.at[p, side, k], halo_rs.at[p, side, k], dev(prv if side == 0 else nxt, z),
        )

    for p in range(2):
        for k in range(nk):
            halo_copy(p, 0, k).start()
            halo_copy(p, 1, k).start()

    for small in smalls:
        small.wait()
    slot = lax.broadcasted_iota(jnp.int32, (1, cols), 1)
    weight = jnp.zeros((1, cols), F32)
    for s in range(cols // cols_per_slice):
        within = slot - s * cols_per_slice
        live = (within >= 0) & (within < counts[s])
        weight = jnp.where(live, jnp.where(within < occupied[s], 2.0, smearing[...].reshape(1, cols)), weight)
    w[...] = weight
    we[...] = weight * energies[...].reshape(1, cols)

    def scaled(block, k):
        at = pl.ds(pl.multiple_of(k * chunk, 128), chunk)
        wide = block.astype(F32)
        return jnp.concatenate(
            [(wide * w[:, at]).astype(BF16), (wide * we[:, at]).astype(BF16)], axis=0
        )

    q[...] = jnp.zeros_like(q)
    cross_a[...] = jnp.zeros_like(cross_a)
    cross_b[...] = jnp.zeros_like(cross_b)
    lstage[...] = jnp.zeros_like(lstage)
    late[...] = jnp.zeros_like(late)
    lxsum[...] = jnp.zeros_like(lxsum)

    def inner(k, carry):
        pltpu.make_async_copy(
            eig.at[:, pl.ds(pl.multiple_of(k * chunk, 128), chunk)], e.at[k], load_sem.at[k]
        ).wait()
        for j in range(nblk):
            lo, hi = max(j - 2, 0), min(j + 3, nblk)
            both = scaled(e[k, j * BS : (j + 1) * BS, :], k)
            if j == nblk - 2:
                sb[0, k] = both
            if j == 1:
                sb[1, k] = both
            got = dot_t(e[k, lo * BS : hi * BS, :], both)
            for i in range(lo, hi):
                q[i * 5 + j - i + 2] += got[(i - lo) * BS : (i - lo + 1) * BS]
        return carry

    lax.fori_loop(0, nk, inner, 0)

    first_block = band * nblk
    for i in range(nblk):
        for j in range(3):
            d = 2 if j == 0 else jnp.clip(block_cols[j, i] - first_block - i + 2, 0, 4)
            block = q[i * 5 + d]
            lanes = slice(j * BS, (j + 1) * BS)
            for o in range(i * BS // own, -(-(i + 1) * BS // own)):
                lo, hi = max(i * BS, own * o), min((i + 1) * BS, own * (o + 1))
                part = block[lo - i * BS : hi - i * BS]
                at = (o % 2, o // 4, o // 2 % 2)
                stage[at + (slice(lo - own * o, hi - own * o), lanes)] = part[:, :BS]
                stage[at + (slice(own + lo - own * o, own + hi - own * o), lanes)] = part[:, BS:]

    pair = remote(stage.at[1 - core], pair_in, pair_ss, pair_rs, dev(band, z, c=1 - core))
    pair.start()

    def outer(p, begin, end):
        def body(k, carry):
            halo_copy(p, 0, k).wait_recv()
            halo_copy(p, 1, k).wait_recv()
            ahead, behind = halo[p, 0, k], halo[p, 1, k]
            cross_a[p, 0] += dot_t(e[k, rows - 2 * BS :, :], scaled(ahead, k))
            cross_b[p, 0] += dot_t(ahead, sb[0, k])
            cross_a[p, 1] += dot_t(e[k, : 2 * BS, :], scaled(behind, k))
            cross_b[p, 1] += dot_t(behind, sb[1, k])
            return carry

        lax.fori_loop(begin, end, body, 0)

    def mine(zz):
        return stage[core, zz] + pair_in[zz]

    def ring_copy(d, t):
        at = (d, t, d) if t == 0 else (d, t)
        return remote(
            rsend.at[at], rrecv.at[at], r_ss.at[d, t], r_rs.at[d, t],
            dev(band, (z + (1 if d == 0 else nz - 1)) % nz),
        )

    def ring(t):
        for d in range(2):
            far = steps - t
            chunk_sum = mine((z + far) % nz if d == 0 else (z + nz - far) % nz)
            if t == 0:
                rsend[d, 0, d] = chunk_sum[d].astype(BF16)
            else:
                ring_copy(d, t - 1).wait_recv()
                if t == 1:
                    rsend[d, 1, 1 - d] = chunk_sum[1 - d].astype(BF16)
                    rsend[d, 1, d] = (chunk_sum[d] + rrecv[d, 0, d].astype(F32)).astype(BF16)
                else:
                    rsend[d, t] = (chunk_sum + rrecv[d, t - 1].astype(F32)).astype(BF16)
            ring_copy(d, t).start()

    def ring_end():
        total = mine(z)
        for d in range(2):
            ring_copy(d, steps - 1).wait_recv()
            if steps == 1:
                xsum[d] = total[d] + rrecv[d, 0, d].astype(F32)
            else:
                total = total + rrecv[d, steps - 1].astype(F32)
        if steps > 1:
            xsum[...] = total

    x_copy = remote(xsum.at[1 - xh], xrecv, x_ss, x_rs, dev(band, z, x=1 - xh))

    def late_pack(p):
        regions = [(s, zz, side, base, 2 * BS, None) for s, zz in enumerate(a_z)
                   for side, base in ((1, 0), (0, rows - 2 * BS))]
        up, dn = b_z[p]
        regions += [(na + 2 * s, zz, 0, HALF * (1 - p), HALF, 0) for s, zz in enumerate(up)]
        regions += [(na + 2 * (len(up) + s), zz, 1, rows - BS + HALF * p, HALF, 0) for s, zz in enumerate(dn)]
        for s, zz, side, base, length, two in regions:
            for o in range(4 * zz, 4 * zz + 4):
                lo, hi = max(base, own * o), min(base + length, own * (o + 1))
                if lo < hi:
                    to = slice(o // 2 % 2 * own + lo - own * o, o // 2 % 2 * own + hi - own * o)
                    if two is None:
                        lstage[p, o % 2, s, to] = cross_a[p, side, lo - base : hi - base]
                    else:
                        lstage[p, o % 2, s, to] = cross_b[p, side, lo - base : hi - base, :BS]
                        lstage[p, o % 2, s + 1, to] = cross_b[p, side, lo - base : hi - base, BS:]

    def late_pair(p):
        return remote(
            lstage.at[p, 1 - core], lpair_in.at[p], lpair_ss.at[p], lpair_rs.at[p],
            dev(band, z, c=1 - core),
        )

    def a_copy(p, s, zz, origin):
        return remote(
            lsend.at[p, s], larecv.at[p, origin], la_ss.at[p, s], la_rs.at[p, origin], dev(band, zz)
        )

    def b_copy(p, s, b, zz, origin):
        return remote(
            lsend.at[p, pl.ds(na + 2 * s, 2)], lbrecv.at[p, origin], lb_ss.at[p, s], lb_rs.at[p, origin],
            dev(b, zz),
        )

    def b_list(p):
        up, dn = b_z[p]
        return [(s, nxt, zz) for s, zz in enumerate(up)] + [
            (len(up) + s, prv, zz) for s, zz in enumerate(dn)
        ]

    def late_send(p):
        late_pair(p).wait_recv()
        lsend[p] = (lstage[p, core] + lpair_in[p]).astype(BF16)
        for s, b, zz in b_list(p):
            b_copy(p, s, b, zz, z).start()
        for s, zz in enumerate(a_z):
            pl.when(z != zz)(a_copy(p, s, zz, z).start)

    is_a = (z < low) | (z >= nz - low)
    is_b = [(z <= max(up)) | (z >= min(dn)) for up, dn in b_z]

    def late_x(p):
        return remote(
            lxsum.at[p, :, pl.ds(pl.multiple_of((1 - xh) * own, 8), own)], lxrecv.at[p],
            lx_ss.at[p], lx_rs.at[p], dev(band, z, x=1 - xh),
        )

    def late_sum(p):
        @pl.when(is_a)
        def _():
            at = jnp.where(z < low, z, z - (nz - na))
            sum_a = lstage[p, core, at] + lpair_in[p, at]
            for k in range(1, nz):
                origin = (z + k) % nz
                a_copy(p, 0, 0, origin).wait_recv()
                sum_a = sum_a + larecv[p, origin].astype(F32)
            lxsum[p, 0] = sum_a

            @pl.when(is_b[p])
            def _():
                sum_b = jnp.zeros(lxsum.shape[2:], F32)[None]
                for k in range(nz):
                    b_copy(p, 0, nxt, 0, k).wait_recv()
                    sum_b = sum_b + lbrecv[p, k].astype(F32)
                lxsum[p, 1:] = sum_b

            late_x(p).start()

    def late_end(p):
        @pl.when(is_a)
        def _():
            late_x(p).wait_recv()
            late[p] = lxsum[p, :, pl.ds(pl.multiple_of(xh * own, 8), own)] + lxrecv[p]

    def cut(part):
        return nk * part // 7

    outer(0, 0, nk)
    pair.wait_recv()
    ring(0)
    late_pack(0)
    late_pair(0).start()
    for t in range(1, steps):
        ring(t)
        outer(1, cut(2 * t - 2), cut(2 * t))
        if t == 1:
            late_send(0)
    if steps == 1:
        late_send(0)
    late_sum(0)
    outer(1, cut(2 * steps - 2), nk)
    late_pack(1)
    late_pair(1).start()
    ring_end()
    x_copy.start()
    late_send(1)
    late_end(0)
    x_copy.wait_recv()
    early = xsum[xh] + xrecv[...]
    late_sum(1)
    late_end(1)

    row_block = (lax.broadcasted_iota(jnp.int32, (own, BS), 0) + own * me) // BS
    top = z < steps
    near = jnp.where(top, late[0, 0], late[1, 0])
    far = jnp.where(top, late[1, 0], late[0, 0])
    for out, start, lanes, row in ((dens, 0, slice(0, HALF), 1), (edens, own, slice(HALF, BS), 2)):
        parts = (
            jnp.concatenate([near[:, lanes], far[:, lanes]], axis=1),
            late[0, row] + late[1, row],
        )
        for j in range(3):
            value = early[start : start + own, j * BS : (j + 1) * BS]
            if j:
                for part, wanted in (
                    (parts[0], ((0, -1), (1, -1), (nblk - 2, nblk), (nblk - 1, nblk))),
                    (parts[1], ((0, -2), (nblk - 1, nblk + 1))),
                ):
                    mask = None
                    for i, rel in wanted:
                        hit = jnp.where(block_cols[j, i] - first_block == rel, i, -1)
                        mask = (row_block == hit) if mask is None else mask | (row_block == hit)
                    value = value + jnp.where(mask, part, 0.0)
            out[:, j * BS : (j + 1) * BS] = value

    pair.wait_send()
    x_copy.wait_send()
    for t in range(steps):
        for d in range(2):
            ring_copy(d, t).wait_send()
    for p in range(2):
        for k in range(nk):
            halo_copy(p, 0, k).wait_send()
            halo_copy(p, 1, k).wait_send()
        late_pair(p).wait_send()
        for s, b, zz in b_list(p):
            b_copy(p, s, b, zz, z).wait_send()
        for s, zz in enumerate(a_z):
            pl.when(z != zz)(a_copy(p, s, zz, z).wait_send)
        pl.when(is_a)(late_x(p).wait_send)


def outer_z(rows, nz):
    rz = rows // nz
    low = -(-2 * BS // rz)
    return list(range(low)) + list(range(nz - low, nz))


def boundary_z(rows, nz, p):
    rz = rows // nz
    base = HALF * (1 - p)
    up = list(range(base // rz, -(-(base + HALF) // rz)))
    base = rows - BS + HALF * p
    return up, list(range(base // rz, -(-(base + HALF) // rz)))


def shards(nband, nz, cols_per_slice, chunk, eigvecs, energies, smearing, counts, occupied, block_cols):
    rows, cols = eigvecs.shape
    nk = cols // chunk
    nblk = rows // BS
    own = rows // (nz * 4)
    na = len(outer_z(rows, nz))
    nb = max(len(up) + len(dn) for up, dn in (boundary_z(rows, nz, p) for p in range(2)))
    nl = na + 2 * nb
    steps = nz // 2
    vmem = pl.BlockSpec(memory_space=pltpu.VMEM)
    dma = pltpu.SemaphoreType.DMA
    wide = 3 * BS
    return pl.pallas_call(
        functools.partial(kernel, nband, nz, cols_per_slice, chunk),
        out_shape=(jax.ShapeDtypeStruct((own, wide), F32),) * 2,
        in_specs=[pl.BlockSpec(memory_space=pl.ANY)] * 6,
        out_specs=(vmem, vmem),
        scratch_shapes=[
            pltpu.VMEM((cols,), F32),
            pltpu.VMEM((cols,), F32),
            pltpu.SMEM(counts.shape, jnp.int32),
            pltpu.SMEM(occupied.shape, jnp.int32),
            pltpu.SMEM((3, nblk), jnp.int32),
            pltpu.VMEM((nk, rows, chunk), BF16),
            pltpu.VMEM((2, 2, nk, HALF, chunk), BF16),
            pltpu.VMEM((1, cols), F32),
            pltpu.VMEM((1, cols), F32),
            pltpu.VMEM((2, nk, 2 * BS, chunk), BF16),
            pltpu.VMEM((nblk * 5, BS, 2 * BS), F32),
            pltpu.VMEM((2, 2, 2 * BS, BS), F32),
            pltpu.VMEM((2, 2, HALF, 2 * BS), F32),
            pltpu.VMEM((2, nz, 2, 2 * own, wide), F32),
            pltpu.VMEM((nz, 2, 2 * own, wide), F32),
            pltpu.VMEM((2, steps, 2, 2 * own, wide), BF16),
            pltpu.VMEM((2, steps, 2, 2 * own, wide), BF16),
            pltpu.VMEM((2, 2 * own, wide), F32),
            pltpu.VMEM((2 * own, wide), F32),
            pltpu.VMEM((2, 2, nl, 2 * own, BS), F32),
            pltpu.VMEM((2, nl, 2 * own, BS), F32),
            pltpu.VMEM((2, nl, 2 * own, BS), BF16),
            pltpu.VMEM((2, nz, 2 * own, BS), BF16),
            pltpu.VMEM((2, nz, 2, 2 * own, BS), BF16),
            pltpu.VMEM((2, 3, 2 * own, BS), F32),
            pltpu.VMEM((2, 3, own, BS), F32),
            pltpu.VMEM((2, 3, own, BS), F32),
            dma((5,)), dma((nk,)), dma((2, 2, nk)), dma((2, 2, nk)), dma, dma,
            dma((2, steps)), dma((2, steps)), dma, dma,
            dma((2,)), dma((2,)), dma((2, na)), dma((2, nz)), dma((2, nb)), dma((2, nz)), dma((2,)), dma((2,)),
        ],
        compiler_params=pltpu.CompilerParams(
            collective_id=0, has_side_effects=True, vmem_limit_bytes=VMEM_LIMIT
        ),
        cost_estimate=pl.CostEstimate(
            flops=2 * 48 * BS * BS * cols, bytes_accessed=rows * cols * 2, transcendentals=0
        ),
    )(eigvecs, energies, smearing, counts, occupied, block_cols.T)


def build(mesh, cols_per_slice, chunk):
    placed = (P("band", "cuts"), P("cuts"), P("cuts"), P("cuts"), P("cuts"), P("band", None))
    body = functools.partial(shards, mesh.shape["band"], mesh.shape["cuts"] // 4, cols_per_slice, chunk)
    return jax.shard_map(
        body,
        mesh=mesh,
        in_specs=placed,
        out_specs=(P(("band", "cuts"), None), P(("band", "cuts"), None)),
        check_vma=False,
    )


def solution(mesh):
    return build(mesh, COLS, CHUNK)
```

time: 62.6 us -> 57.6 us (0.920)
  local copies, waits for them, and re-layouts: 7.33 us -> 2.77 us
    unnamed x9 -> x2, local copies, waits for them, and re-layouts: 5.87 us -> 2.77 us
    reshape x2 -> x0, local copies, waits for them, and re-layouts: 1.46 us -> none  [the longest x1 0.73 us: shards(): smearing.reshape(1, cols)]
where the time goes in v2:
time: 57.6 us; the launch traced here: 57.2 us
  Pallas kernels  53.8 us (93%)
  local copies, waits for them, and re-layouts  2.77 us (5%)
  between operations  0.64 us (1%)
    pallas_call x1, Pallas kernels, shards(): pl.pallas_call(functools.partial(kernel, nband, nz, cols_per_slice, chunk...  53.8 us
    unnamed x2, local copies, waits for them, and re-layouts  2.77 us

profile of v2, /device:TPU:1, one launch (start us, length us, event | category | flops | bytes accessed | tf_op | source)
XLA Modules:
  0.0 57.2 jit_solution(15568437983062785422)
XLA Ops:
  0.6 53.8 %shard_map.77 = (f32[24,384]{1,0:T(8,128)}, f32[24,384]{1,0:T(8,128)}) custom-call(bf16[768,3584]{1,0:T(8,128)(2,1)} %eig.1, f32[3584]{0:T(1024)} %energies_in.1, f32[3584]{0:T(1024)} %smearing_in.1, s32[2]{0:T(128)} %counts_in.1, s32[2]{0:T(128)} %occupied_in.1, s32[3,6]{1,0:T(4,128)} %bitcast.1), custom_call_target="tpu_custom_call" | custom-call | flops 5637144576 | bytes 5505024 | tf_op jit(solution)/shard_map/pallas_call | solution.py:395
  54.5 1.4 %copy.10 = f32[24,384]{1,0:T(8,128)} copy(f32[24,384]{1,0:T(8,128)} %get-tuple-element.4) | data formatting | bytes 73728
  55.8 1.4 %copy.11 = f32[24,384]{1,0:T(8,128)} copy(f32[24,384]{1,0:T(8,128)} %get-tuple-element.5) | data formatting | bytes 73728

commit v3 on v2

v3 whole, which is shorter than its diff:
```python
import functools

import jax
import jax.numpy as jnp
from jax import lax
from jax.experimental import pallas as pl
from jax.experimental.pallas import tpu as pltpu
from jax.sharding import PartitionSpec as P

BS = 128
COLS = 1792
CHUNK = 512
SPLIT = ((0, 96), (96, 32))
VMEM_LIMIT = 60 * 1024 * 1024
MESH = pl.DeviceIdType.MESH
F32, BF16 = jnp.float32, jnp.bfloat16


def dot_t(a, b):
    return lax.dot_general(a, b, (((1,), (1,)), ((), ())), preferred_element_type=F32)


def kernel(
    nband, nz, cols_per_slice, chunk,
    eig, energies_in, smearing_in, counts_in, occupied_in, cols_in, dens, edens,
    energies, smearing, counts, occupied, block_cols, e, w, we, ss, q,
    halo0, halo1, cross_a0, cross_a1, cross_b0, cross_b1,
    stage0, stage1, pair0, pair1, rsend0, rsend1, rrecv0, rrecv1, xsum, xrecv,
    lstage0, lstage1, lpair0, lpair1, lsend0, lsend1, larecv0, larecv1, lbrecv0, lbrecv1,
    lxsum, lxrecv, late_a0, late_a1, late_b,
    wave, ready, small_sem, load_sem, halo_ss, halo_rs, pair_ss, pair_rs, r_ss, r_rs, x_ss, x_rs,
    lpair_ss, lpair_rs, la_ss, la_rs, lb_ss, lb_rs, lx_ss, lx_rs,
):
    rows, cols = eig.shape
    nk = cols // chunk
    nblk = rows // BS
    own = dens.shape[0]
    hr = packed_rows(own)
    ng = 2 * nz
    halo, cross_a, cross_b = (halo0, halo1), (cross_a0, cross_a1), (cross_b0, cross_b1)
    lstage, lpair_in, lsend = (lstage0, lstage1), (lpair0, lpair1), (lsend0, lsend1)
    larecv, lbrecv = (larecv0, larecv1), (lbrecv0, lbrecv1)
    stage, pair_in, rsend, rrecv = (stage0, stage1), (pair0, pair1), (rsend0, rsend1), (rrecv0, rrecv1)
    a_rows = (2 * own, hr)
    a_g = outer_groups(rows, nz)
    na = len(a_g)
    b_g = [boundary_groups(rows, nz, p) for p in range(2)]

    me = lax.axis_index("cuts")
    band = lax.axis_index("band")
    g, core = me // 2, me % 2
    z, xh = g // 2, g % 2
    nxt, prv = (band + 1) % nband, (band + nband - 1) % nband

    def dev(b, gg):
        return {"cuts": gg * 2 + core, "band": b}

    across = {"cuts": z * 4 + (1 - xh) * 2 + core, "band": band}
    partner = {"cuts": g * 2 + 1 - core, "band": band}

    def remote(src, dst, send_sem, recv_sem, device):
        return pltpu.make_async_remote_copy(
            src_ref=src, dst_ref=dst, send_sem=send_sem, recv_sem=recv_sem,
            device_id=device, device_id_type=MESH,
        )

    barrier = pltpu.get_barrier_semaphore()

    def greet(device):
        pl.semaphore_signal(barrier, inc=1, device_id=device, device_id_type=MESH)

    greet(dev(nxt, g))
    greet(dev(prv, g))
    ring = (dev(band, (z + 1) % nz * 2 + xh), dev(band, (z + nz - 1) % nz * 2 + xh))
    greet(ring[0])
    greet(ring[1])
    greet(across)
    greet(partner)

    smalls = []
    for t, (src, dst) in enumerate((
        (energies_in, energies), (smearing_in, smearing),
        (counts_in, counts), (occupied_in, occupied), (cols_in, block_cols),
    )):
        small = pltpu.make_async_copy(src, dst, small_sem.at[t])
        small.start()
        smalls.append(small)
    for k in range(nk):
        pltpu.make_async_copy(eig.at[:, pl.ds(k * chunk, chunk)], e.at[k], load_sem.at[k]).start()

    pl.semaphore_wait(barrier, 6)

    def halo_copy(p, side, k):
        q0, n = SPLIT[p]
        first = q0 if side == 0 else rows - BS + q0
        start = k * chunk if isinstance(k, int) else pl.multiple_of(k * chunk, 128)
        return remote(
            eig.at[pl.ds(first, n), pl.ds(start, chunk)], halo[p].at[side, k],
            halo_ss.at[p, side, k], halo_rs.at[p, side, k], dev(prv if side == 0 else nxt, g),
        )

    for p in range(2):
        for k in range(nk):
            halo_copy(p, 0, k).start()
            halo_copy(p, 1, k).start()

    def tell(sem, device):
        pl.semaphore_signal(sem, inc=1, device_id=device, device_id_type=MESH)

    def relay(t):
        for d in range(2):
            if t:
                pl.semaphore_wait(wave.at[d, t - 1], 1)
            if t < nz // 2:
                tell(wave.at[d, t], ring[d])
            elif d == 1:
                tell(ready.at[0], dev(nxt, g))
                tell(ready.at[1], dev(prv, g))

    relay(0)
    for small in smalls:
        small.wait()
    slot = lax.broadcasted_iota(jnp.int32, (1, cols), 1)
    weight = jnp.zeros((1, cols), F32)
    for s in range(cols // cols_per_slice):
        within = slot - s * cols_per_slice
        live = (within >= 0) & (within < counts[s])
        weight = jnp.where(live, jnp.where(within < occupied[s], 2.0, smearing[...].reshape(1, cols)), weight)
    w[...] = weight
    we[...] = weight * energies[...].reshape(1, cols)

    def scaled(block, k, pad=0):
        at = pl.ds(pl.multiple_of(k * chunk, 128), chunk)
        wide = block.astype(F32)
        parts = [(wide * w[:, at]).astype(BF16), (wide * we[:, at]).astype(BF16)]
        if pad:
            gap = jnp.zeros((pad, chunk), BF16)
            parts = [parts[0], gap, parts[1], gap]
        return jnp.concatenate(parts, axis=0)

    for ref in (q, cross_a0, cross_a1, cross_b0, cross_b1, lstage0, lstage1, lxsum, late_a0, late_a1, late_b):
        ref[...] = jnp.zeros_like(ref)

    def diagonal(k, carry):
        pltpu.make_async_copy(
            eig.at[:, pl.ds(pl.multiple_of(k * chunk, 128), chunk)], e.at[k], load_sem.at[k]
        ).wait()
        for j in range(nblk):
            block = e[k, j * BS : (j + 1) * BS, :]
            both = scaled(block, k)
            ss[j, k] = both
            q[j * 5 + 2] += dot_t(block, both)
        return carry

    def others(k, carry):
        for j in range(nblk):
            near = [i for i in range(max(j - 2, 0), min(j + 3, nblk)) if i != j]
            left = jnp.concatenate([e[k, i * BS : (i + 1) * BS, :] for i in near], axis=0)
            got = dot_t(left, ss[j, k])
            for t, i in enumerate(near):
                q[i * 5 + j - i + 2] += got[t * BS : (t + 1) * BS]
        return carry

    first_block = band * nblk

    def early_pack(h):
        for i in range(nblk):
            for j in ((0,), (1, 2))[h]:
                d = 2 if j == 0 else jnp.clip(block_cols[j, i] - first_block - i + 2, 0, 4)
                block = q[i * 5 + d]
                lanes = slice((j - h) * BS, (j - h + 1) * BS)
                for o in range(i * BS // own, -(-(i + 1) * BS // own)):
                    lo, hi = max(i * BS, own * o), min((i + 1) * BS, own * (o + 1))
                    part = block[lo - i * BS : hi - i * BS]
                    at = (o % 2, o // 2)
                    stage[h][at + (slice(lo - own * o, hi - own * o), lanes)] = part[:, :BS]
                    stage[h][at + (slice(own + lo - own * o, own + hi - own * o), lanes)] = part[:, BS:]

    def early_pair(h):
        return remote(stage[h].at[1 - core], pair_in[h], pair_ss.at[h], pair_rs.at[h], partner)

    hops = nz // 2

    def mine(h, zz):
        at = pl.ds(2 * zz, 2)
        return stage[h][core, at] + pair_in[h][at]

    def ring_copy(h, d, t):
        at = (d, t, d) if t == 0 else (d, t)
        return remote(rsend[h].at[at], rrecv[h].at[at], r_ss.at[h, d, t], r_rs.at[h, d, t], ring[d])

    def pass_on(h, t):
        for d in range(2):
            far = hops - t
            part = mine(h, (z + far) % nz if d == 0 else (z + nz - far) % nz)
            if t == 0:
                rsend[h][d, 0, d] = part[d].astype(BF16)
            else:
                ring_copy(h, d, t - 1).wait_recv()
                if t == 1:
                    rsend[h][d, 1, 1 - d] = part[1 - d].astype(BF16)
                    rsend[h][d, 1, d] = (part[d] + rrecv[h][d, 0, d].astype(F32)).astype(BF16)
                else:
                    rsend[h][d, t] = (part + rrecv[h][d, t - 1].astype(F32)).astype(BF16)
            ring_copy(h, d, t).start()

    def ring_end(h):
        total = mine(h, z)
        for d in range(2):
            ring_copy(h, d, hops - 1).wait_recv()
            if hops > 1:
                total = total + rrecv[h][d, hops - 1].astype(F32)
        lanes = slice(h * BS, (1 + 2 * h) * BS)
        for d in range(2):
            xsum[d, :, lanes] = total[d] if hops > 1 else total[d] + rrecv[h][d, 0, d].astype(F32)

    x_copy = remote(xsum.at[1 - xh], xrecv, x_ss, x_rs, across)

    def outer(p, begin, end):
        pad = BS - SPLIT[p][1] if p == 0 else 0

        def body(k, carry):
            halo_copy(p, 0, k).wait_recv()
            halo_copy(p, 1, k).wait_recv()
            ahead, behind = halo[p][0, k], halo[p][1, k]
            cross_a[p][0] += dot_t(e[k, rows - 2 * BS :, :], scaled(ahead, k, pad))
            cross_b[p][0] += dot_t(ahead, ss[nblk - 2, k])
            cross_a[p][1] += dot_t(e[k, : 2 * BS, :], scaled(behind, k, pad))
            cross_b[p][1] += dot_t(behind, ss[1, k])
            return carry

        lax.fori_loop(begin, end, body, 0)

    def late_pack(p):
        stored = lstage[p]
        q0, n = SPLIT[p]
        for s, gg in enumerate(a_g):
            for o in (2 * gg, 2 * gg + 1):
                for side, base in ((1, 0), (0, rows - 2 * BS)):
                    lo, hi = max(base, own * o), min(base + 2 * BS, own * (o + 1))
                    if lo >= hi:
                        continue
                    a, b = lo - own * o, hi - own * o
                    off = s * a_rows[p]
                    if p == 0:
                        part = cross_a[0][side, lo - base : hi - base]
                        stored[o % 2, off + a : off + b] = part[:, :BS]
                        stored[o % 2, off + own + a : off + own + b] = part[:, BS:]
                    else:
                        for x0, x1, lane in ((a, min(b, hr), 0), (max(a, hr), b, BS // 2)):
                            if x0 < x1:
                                from_row = lo - base - a
                                shift = off - (hr if lane else 0)
                                stored[o % 2, shift + x0 : shift + x1, lane : lane + BS // 2] = cross_a[1][
                                    side, from_row + x0 : from_row + x1
                                ]
        up, dn = b_g[p]
        todo = [(s, gg, 0, q0) for s, gg in enumerate(up)]
        todo += [(len(up) + s, gg, 1, rows - BS + q0) for s, gg in enumerate(dn)]
        for s, gg, side, base in todo:
            for o in (2 * gg, 2 * gg + 1):
                lo, hi = max(base, own * o), min(base + n, own * (o + 1))
                if lo < hi:
                    off = na * a_rows[p] + 2 * own * s
                    a, b = lo - own * o, hi - own * o
                    part = cross_b[p][side, lo - base : hi - base]
                    stored[o % 2, off + a : off + b] = part[:, :BS]
                    stored[o % 2, off + own + a : off + own + b] = part[:, BS:]

    def late_pair(p):
        return remote(lstage[p].at[1 - core], lpair_in[p], lpair_ss.at[p], lpair_rs.at[p], partner)

    def a_copy(p, s, gg, origin):
        size = a_rows[p] * (2 - p)
        return remote(
            lsend[p].at[pl.ds(s * size, size)], larecv[p].at[origin],
            la_ss.at[p, s], la_rs.at[p, origin], dev(band, 2 * gg + xh if p == 0 else gg),
        )

    def b_copy(p, s, b, gg, origin):
        size = 2 * own * (2 - p)
        return remote(
            lsend[p].at[pl.ds(na * a_rows[p] + s * size, size)], lbrecv[p].at[origin],
            lb_ss.at[p, s], lb_rs.at[p, origin], dev(b, 2 * gg + xh if p == 0 else gg),
        )

    def a_list(p):
        return list(enumerate(a_g if p else [t // 2 for t in a_g[::2]]))

    def b_list(p):
        up, dn = b_g[p] if p else [[t // 2 for t in part[::2]] for part in b_g[0]]
        return [(s, nxt, gg) for s, gg in enumerate(up)] + [
            (len(up) + s, prv, gg) for s, gg in enumerate(dn)
        ]

    def late_send(p):
        late_pair(p).wait_recv()
        lsend[p][...] = (lstage[p][core] + lpair_in[p][...]).astype(BF16)
        here = g if p else z
        for s, b, gg in b_list(p):
            b_copy(p, s, b, gg, here).start()
        for s, gg in a_list(p):
            pl.when(here != gg)(a_copy(p, s, gg, here).start)

    low = na // 2
    is_a = (g < low) | (g >= ng - low)

    def within_groups(p):
        up, dn = b_g[p]
        return ((g >= up[0]) & (g <= up[-1])) | ((g >= dn[0]) & (g <= dn[-1]))

    lx = remote(lxsum.at[:, 1 - xh], lxrecv, lx_ss, lx_rs, across)

    def late_sum0():
        @pl.when(is_a)
        def _():
            size = 4 * own
            at = pl.ds(pl.multiple_of(jnp.where(g < low, z, z - (nz - na // 2)) * size, 16), size)
            total = lstage0[core, at] + lpair0[at]
            for k in range(1, nz):
                origin = (z + k) % nz
                a_copy(0, 0, 0, origin).wait_recv()
                total = total + larecv0[origin].astype(F32)
            lxsum[0, 0] = total[: 2 * own]
            lxsum[0, 1] = total[2 * own :]

            @pl.when(within_groups(0))
            def _():
                total = jnp.zeros((4 * own, BS), F32)
                for k in range(nz):
                    b_copy(0, 0, nxt, 0, k).wait_recv()
                    total = total + lbrecv0[k].astype(F32)
                lxsum[1, 0] = total[: 2 * own]
                lxsum[1, 1] = total[2 * own :]

            lx.start()

    def late_end0():
        @pl.when(is_a)
        def _():
            lx.wait_recv()
            late_a0[...] = lxsum[0, xh] + lxrecv[0]
            late_b[...] += lxsum[1, xh] + lxrecv[1]

    def late_sum1():
        @pl.when(is_a)
        def _():
            at = pl.ds(pl.multiple_of(jnp.where(g < low, g, g - (ng - na)) * hr, 16), hr)
            total = lstage1[core, at] + lpair1[at]
            for k in range(1, ng):
                origin = (g + k) % ng
                a_copy(1, 0, 0, origin).wait_recv()
                total = total + larecv1[origin].astype(F32)
            late_a1[...] = total

        @pl.when(within_groups(1))
        def _():
            total = late_b[...]
            for k in range(ng):
                b_copy(1, 0, nxt, 0, k).wait_recv()
                total = total + lbrecv1[k].astype(F32)
            late_b[...] = total

    def cut(part):
        return nk * part // 7

    def more(begin, end):
        lax.fori_loop(cut(begin), cut(end), others, 0)

    lax.fori_loop(0, nk, diagonal, 0)
    early_pack(0)
    early_pair(0).start()
    more(0, 2)
    if hops > 1:
        relay(1)
    early_pair(0).wait_recv()
    pass_on(0, 0)
    more(2, 4)
    if hops > 2:
        relay(2)
    more(4, 6)
    for t in range(3, hops):
        relay(t)
    if hops > 1:
        pass_on(0, 1)
    more(6, 7)
    early_pack(1)
    early_pair(1).start()
    outer(0, 0, cut(2))
    if hops > 2:
        pass_on(0, 2)
    early_pair(1).wait_recv()
    pass_on(1, 0)
    outer(0, cut(2), cut(4))
    for t in range(3, hops):
        pass_on(0, t)
    if hops > 1:
        pass_on(1, 1)
    outer(0, cut(4), nk)
    late_pack(0)
    late_pair(0).start()
    ring_end(0)
    relay(hops)
    outer(1, 0, cut(3))
    if hops > 2:
        pass_on(1, 2)
    pl.semaphore_wait(ready.at[0], 1)
    pl.semaphore_wait(ready.at[1], 1)
    late_send(0)
    outer(1, cut(3), cut(5))
    for t in range(3, hops):
        pass_on(1, t)
    outer(1, cut(5), nk)
    late_pack(1)
    late_pair(1).start()
    late_send(1)
    ring_end(1)
    x_copy.start()
    late_sum0()
    late_sum1()
    late_end0()
    x_copy.wait_recv()
    early = xsum[xh] + xrecv[...]

    row_block = (lax.broadcasted_iota(jnp.int32, (own, BS), 0) + own * me) // BS
    n0, n1 = SPLIT[0][1], SPLIT[1][1]
    packed = late_a1[...]
    tail = jnp.concatenate([packed[:, : BS // 2], packed[: own - hr, BS // 2 :]], axis=0)
    for out, start, lane in ((dens, 0, 0), (edens, own, n1)):
        rows_here = slice(start, start + own)
        parts = (
            jnp.concatenate([late_a0[rows_here, :n0], tail[:, lane : lane + n1]], axis=1),
            late_b[rows_here],
        )
        for j in range(3):
            value = early[rows_here, j * BS : (j + 1) * BS]
            if j:
                for part, wanted in (
                    (parts[0], ((0, -1), (1, -1), (nblk - 2, nblk), (nblk - 1, nblk))),
                    (parts[1], ((0, -2), (nblk - 1, nblk + 1))),
                ):
                    mask = None
                    for i, rel in wanted:
                        hit = jnp.where(block_cols[j, i] - first_block == rel, i, -1)
                        mask = (row_block == hit) if mask is None else mask | (row_block == hit)
                    value = value + jnp.where(mask, part, 0.0)
            out[:, j * BS : (j + 1) * BS] = value

    for h in range(2):
        early_pair(h).wait_send()
        for t in range(hops):
            for d in range(2):
                ring_copy(h, d, t).wait_send()
    x_copy.wait_send()
    for p in range(2):
        for k in range(nk):
            halo_copy(p, 0, k).wait_send()
            halo_copy(p, 1, k).wait_send()
        late_pair(p).wait_send()
        here = g if p else z
        for s, b, gg in b_list(p):
            b_copy(p, s, b, gg, here).wait_send()
        for s, gg in a_list(p):
            pl.when(here != gg)(a_copy(p, s, gg, here).wait_send)
    pl.when(is_a)(lx.wait_send)


def packed_rows(own):
    return -(-own // 32) * 16


def outer_groups(rows, nz):
    low = -(-2 * BS // (rows // (2 * nz)))
    return list(range(low)) + list(range(2 * nz - low, 2 * nz))


def boundary_groups(rows, nz, p):
    per = rows // (2 * nz)
    q0, n = SPLIT[p]
    last = rows - BS + q0
    up, dn = (q0 // per, -(-(q0 + n) // per)), (last // per, -(-(last + n) // per))
    if p == 0:
        up, dn = ((a // 2 * 2, -(-b // 2) * 2) for a, b in (up, dn))
    return list(range(*up)), list(range(*dn))


def shards(nband, nz, cols_per_slice, chunk, eigvecs, energies, smearing, counts, occupied, block_cols):
    rows, cols = eigvecs.shape
    nk = cols // chunk
    nblk = rows // BS
    own = rows // (nz * 4)
    ng = 2 * nz
    hr = packed_rows(own)
    na = len(outer_groups(rows, nz))
    nb = [len(up) + len(dn) for up, dn in (boundary_groups(rows, nz, p) for p in range(2))]
    late0 = (na + nb[0]) * 2 * own
    late1 = na * hr + nb[1] * 2 * own
    n0, n1 = SPLIT[0][1], SPLIT[1][1]
    vmem = pl.BlockSpec(memory_space=pltpu.VMEM)
    dma = pltpu.SemaphoreType.DMA
    wide = 3 * BS
    return pl.pallas_call(
        functools.partial(kernel, nband, nz, cols_per_slice, chunk),
        out_shape=(jax.ShapeDtypeStruct((own, wide), F32),) * 2,
        in_specs=[pl.BlockSpec(memory_space=pl.ANY)] * 6,
        out_specs=(vmem, vmem),
        scratch_shapes=[
            pltpu.VMEM((cols,), F32),
            pltpu.VMEM((cols,), F32),
            pltpu.SMEM(counts.shape, jnp.int32),
            pltpu.SMEM(occupied.shape, jnp.int32),
            pltpu.SMEM((3, nblk), jnp.int32),
            pltpu.VMEM((nk, rows, chunk), BF16),
            pltpu.VMEM((1, cols), F32),
            pltpu.VMEM((1, cols), F32),
            pltpu.VMEM((nblk, nk, 2 * BS, chunk), BF16),
            pltpu.VMEM((nblk * 5, BS, 2 * BS), F32),
            pltpu.VMEM((2, nk, n0, chunk), BF16),
            pltpu.VMEM((2, nk, n1, chunk), BF16),
            pltpu.VMEM((2, 2 * BS, 2 * BS), F32),
            pltpu.VMEM((2, 2 * BS, 2 * n1), F32),
            pltpu.VMEM((2, n0, 2 * BS), F32),
            pltpu.VMEM((2, n1, 2 * BS), F32),
            pltpu.VMEM((2, ng, 2 * own, BS), F32),
            pltpu.VMEM((2, ng, 2 * own, 2 * BS), F32),
            pltpu.VMEM((ng, 2 * own, BS), F32),
            pltpu.VMEM((ng, 2 * own, 2 * BS), F32),
            pltpu.VMEM((2, nz // 2, 2, 2 * own, BS), BF16),
            pltpu.VMEM((2, nz // 2, 2, 2 * own, 2 * BS), BF16),
            pltpu.VMEM((2, nz // 2, 2, 2 * own, BS), BF16),
            pltpu.VMEM((2, nz // 2, 2, 2 * own, 2 * BS), BF16),
            pltpu.VMEM((2, 2 * own, wide), F32),
            pltpu.VMEM((2 * own, wide), F32),
            pltpu.VMEM((2, late0, BS), F32),
            pltpu.VMEM((2, late1, BS), F32),
            pltpu.VMEM((late0, BS), F32),
            pltpu.VMEM((late1, BS), F32),
            pltpu.VMEM((late0, BS), BF16),
            pltpu.VMEM((late1, BS), BF16),
            pltpu.VMEM((nz, 4 * own, BS), BF16),
            pltpu.VMEM((ng, hr, BS), BF16),
            pltpu.VMEM((nz, 4 * own, BS), BF16),
            pltpu.VMEM((ng, 2 * own, BS), BF16),
            pltpu.VMEM((2, 2, 2 * own, BS), F32),
            pltpu.VMEM((2, 2 * own, BS), F32),
            pltpu.VMEM((2 * own, BS), F32),
            pltpu.VMEM((hr, BS), F32),
            pltpu.VMEM((2 * own, BS), F32),
            pltpu.SemaphoreType.REGULAR((2, nz // 2)), pltpu.SemaphoreType.REGULAR((2,)),
            dma((5,)), dma((nk,)), dma((2, 2, nk)), dma((2, 2, nk)), dma((2,)), dma((2,)),
            dma((2, 2, nz // 2)), dma((2, 2, nz // 2)), dma, dma,
            dma((2,)), dma((2,)), dma((2, na)), dma((2, ng)), dma((2, max(nb))), dma((2, ng)), dma, dma,
        ],
        compiler_params=pltpu.CompilerParams(
            collective_id=0, has_side_effects=True, vmem_limit_bytes=VMEM_LIMIT
        ),
        cost_estimate=pl.CostEstimate(
            flops=2 * 48 * BS * BS * cols, bytes_accessed=rows * cols * 2, transcendentals=0
        ),
    )(eigvecs, energies, smearing, counts, occupied, block_cols.T)


def build(mesh, cols_per_slice, chunk):
    placed = (P("band", "cuts"), P("cuts"), P("cuts"), P("cuts"), P("cuts"), P("band", None))
    body = functools.partial(shards, mesh.shape["band"], mesh.shape["cuts"] // 4, cols_per_slice, chunk)
    return jax.shard_map(
        body,
        mesh=mesh,
        in_specs=placed,
        out_specs=(P(("band", "cuts"), None), P(("band", "cuts"), None)),
        check_vma=False,
    )


def solution(mesh):
    return build(mesh, COLS, CHUNK)
```

time: 57.6 us -> 52.9 us (0.918)
  Pallas kernels: 53.8 us -> 48.5 us
    pallas_call x1, Pallas kernels: 53.8 us -> 48.5 us  [shards(): pl.pallas_call(functools.partial(kernel, nband, nz, cols_per_slice, chunk...]
where the time goes in v3:
time: 52.9 us; the launch traced here: 52 us
  Pallas kernels  48.5 us (92%)
  local copies, waits for them, and re-layouts  2.77 us (5%)
  between operations  0.64 us (1%)
    pallas_call x1, Pallas kernels, shards(): pl.pallas_call(functools.partial(kernel, nband, nz, cols_per_slice, chunk...  48.5 us
    unnamed x2, local copies, waits for them, and re-layouts  2.77 us

profile of v3, /device:TPU:1, one launch (start us, length us, event | category | flops | bytes accessed | tf_op | source)
XLA Modules:
  0.0 52.0 jit_solution(9879531244681664854)
XLA Ops:
  0.6 48.5 %shard_map.77 = (f32[24,384]{1,0:T(8,128)}, f32[24,384]{1,0:T(8,128)}) custom-call(bf16[768,3584]{1,0:T(8,128)(2,1)} %eig.1, f32[3584]{0:T(1024)} %energies_in.1, f32[3584]{0:T(1024)} %smearing_in.1, s32[2]{0:T(128)} %counts_in.1, s32[2]{0:T(128)} %occupied_in.1, s32[3,6]{1,0:T(4,128)} %bitcast.1), custom_call_target="tpu_custom_call" | custom-call | flops 5637144576 | bytes 5505024 | tf_op jit(solution)/shard_map/pallas_call | solution.py:502
  49.2 1.4 %copy.10 = f32[24,384]{1,0:T(8,128)} copy(f32[24,384]{1,0:T(8,128)} %get-tuple-element.4) | data formatting | bytes 73728
  50.6 1.4 %copy.11 = f32[24,384]{1,0:T(8,128)} copy(f32[24,384]{1,0:T(8,128)} %get-tuple-element.5) | data formatting | bytes 73728

commit v4 on v3

--- a/solution.py
+++ b/solution.py
@@ -9,7 +9,7 @@
 
 BS = 128
 COLS = 1792
-CHUNK = 512
+CHUNK = 896
 SPLIT = ((0, 96), (96, 32))
 VMEM_LIMIT = 60 * 1024 * 1024
 MESH = pl.DeviceIdType.MESH

time: 52.9 us -> 52.4 us (level); the launches traced: 52 us -> 52.2 us
  no operation moved by 1% of the time
where the time goes in v4:
time: 52.4 us; the launch traced here: 52.2 us
  Pallas kernels  48.8 us (93%)
  local copies, waits for them, and re-layouts  2.77 us (5%)
  between operations  0.64 us (1%)
    pallas_call x1, Pallas kernels, shards(): pl.pallas_call(functools.partial(kernel, nband, nz, cols_per_slice, chunk...  48.8 us
    unnamed x2, local copies, waits for them, and re-layouts  2.77 us

profile of v4, /device:TPU:1, one launch (start us, length us, event | category | flops | bytes accessed | tf_op | source)
XLA Modules:
  0.0 52.2 jit_solution(3261113132508746490)
XLA Ops:
  0.6 48.8 %shard_map.77 = (f32[24,384]{1,0:T(8,128)}, f32[24,384]{1,0:T(8,128)}) custom-call(bf16[768,3584]{1,0:T(8,128)(2,1)} %eig.1, f32[3584]{0:T(1024)} %energies_in.1, f32[3584]{0:T(1024)} %smearing_in.1, s32[2]{0:T(128)} %counts_in.1, s32[2]{0:T(128)} %occupied_in.1, s32[3,6]{1,0:T(4,128)} %bitcast.1), custom_call_target="tpu_custom_call" | custom-call | flops 5637144576 | bytes 5505024 | tf_op jit(solution)/shard_map/pallas_call | solution.py:502
  49.4 1.4 %copy.10 = f32[24,384]{1,0:T(8,128)} copy(f32[24,384]{1,0:T(8,128)} %get-tuple-element.4) | data formatting | bytes 73728
  50.8 1.4 %copy.11 = f32[24,384]{1,0:T(8,128)} copy(f32[24,384]{1,0:T(8,128)} %get-tuple-element.5) | data formatting | bytes 73728
